TPU v7x, 256 devices: a whole 4x4x8 slice. The times are simulated.
256 devices in a mesh: freq: 16 (over y_lo, z), obs: 16 (over x, y_hi, core).
Axes of the slice: x: 4, y: 4 (y_hi: 2, y_lo: 2; y = y_hi * 2 + y_lo), z: 8, core: 2. Of those that a mesh axis runs over, the one named last changes fastest.
Arguments:
- samples: bfloat16 [4, 2048, 8192], P(None, 'freq', 'obs'), may hold values from -6 to 6
- panel_geom: float32 [4, 8192], P(None, 'obs'), may hold values from -1 to 2, as said below
- panel_slot: int32 [16, 512], P('obs'), may hold values from 0 to 511, each once within a row
- observer_pos: float32 [3, 4096], P(None, 'obs'), may hold values from -4 to 4, as said below
- observer_slot: int32 [16, 256], P('obs'), may hold values from 0 to 255, each once within a row
Outputs:
- pressure: float32 [4096, 64, 2, 16], P('obs', 'freq')
Inputs may be any that keep to these rules, and one draw needn't show every extreme that they name: `panel_geom`: panel centres lie in the cube of half side 1 about the anchor; areas lie in 0.5 to 2. `observer_pos`: observers lie between radius 2.5 and 4 from the anchor. `panel_slot`: each row is a reordering of 0 to 511. `observer_slot`: each row is a reordering of 0 to 255.
All inputs are finite; a program needn't handle non-finite values.
Results may differ from a plain program's by a relative error of at most 0.0051.
Values may be sent and summed in bfloat16 or wider, within the bound.
A program may use at most 64 MiB of HBM per device.

v0:
```python
import math

import jax
import jax.numpy as jnp
from jax import lax
from jax.sharding import PartitionSpec as P

WIN = 128
FREQS = 64


def dft_table(window, count):
    step_index = jnp.arange(window, dtype=jnp.int32)
    bin_index = jnp.arange(1, count + 1, dtype=jnp.int32)
    residue = bin_index[:, None] * step_index[None, :] % window
    angles = 2.0 * math.pi / window * residue.astype(jnp.float32)
    hann_window = 0.5 - 0.5 * jnp.cos(2.0 * math.pi / window * step_index.astype(jnp.float32))
    norm_factor = 1.0 / jnp.sqrt(jnp.sum(hann_window * hann_window))
    weighted = hann_window[None, :] * norm_factor
    return jnp.concatenate([jnp.cos(angles) * weighted, -jnp.sin(angles) * weighted], 0).astype(
        jnp.bfloat16
    )


def green_tile(listeners, geometry, wavenumber, scale):
    delta = listeners[:, :, None] - geometry[:3, None, :]
    distance = jnp.sqrt(jnp.sum(delta * delta, axis=0))
    inverse = 1.0 / distance
    direction = delta * inverse
    weights = geometry[3][None, :] * scale
    wave_col = wavenumber[:, None, None]
    phases = wave_col * distance
    green_re = jnp.cos(phases) * inverse * (0.25 / math.pi)
    green_im = -jnp.sin(phases) * inverse * (0.25 / math.pi)
    mono_re = wave_col * green_im * weights
    mono_im = -wave_col * green_re * weights
    dip_re = (green_re * inverse - wave_col * green_im) * weights
    dip_im = (green_im * inverse + wave_col * green_re) * weights
    pieces = [jnp.stack([mono_re, mono_im], 2)]
    for axis_id in range(3):
        pieces.append(jnp.stack([dip_re * direction[axis_id], dip_im * direction[axis_id]], 2))
    return jnp.stack(pieces, 2).astype(jnp.bfloat16)


def source_sides(spectra):
    real_part = spectra[0]
    imag_part = spectra[1]
    first = jnp.stack([real_part, -imag_part], 2)
    second = jnp.stack([imag_part, real_part], 2)
    return jnp.stack([first, second], 1)


def contribution(listeners, geometry, spectra, wavenumber, scale):
    width = geometry.shape[-1]
    block_width = min(width, 512)
    block_count = width // block_width
    start_value = jnp.zeros(
        (listeners.shape[1], spectra.shape[1], 2, spectra.shape[3]), jnp.float32
    )

    def add_block(running, block_id):
        geom_block = lax.dynamic_slice_in_dim(geometry, block_id * block_width, block_width, 1)
        spec_block = lax.dynamic_slice_in_dim(spectra, block_id * block_width, block_width, 4)
        tile = green_tile(listeners, geom_block, wavenumber, scale)
        sides = source_sides(spec_block)
        return (
            running
            + jnp.einsum("focxp,fzcxgp->ofzg", tile, sides, preferred_element_type=jnp.float32),
            None,
        )

    result, _ = lax.scan(add_block, start_value, jnp.arange(block_count, dtype=jnp.int32))
    return result


def local(samples, panel_geom, panel_slot, observer_pos, observer_slot):
    channels, local_steps, panel_count = samples.shape
    segs_here = local_steps // WIN
    table = dft_table(WIN, FREQS)
    records = samples.reshape(channels, segs_here, WIN, panel_count)
    spectra = jnp.einsum("qw,cgwp->qcgp", table, records, preferred_element_type=jnp.float32)
    spectra = spectra.reshape(2, FREQS, channels, segs_here, panel_count).astype(jnp.bfloat16)
    spectra = lax.all_to_all(spectra, "freq", split_axis=1, concat_axis=3, tiled=True)
    bins_here = spectra.shape[1]
    bin_number = lax.axis_index("freq") * bins_here + jnp.arange(1, bins_here + 1, dtype=jnp.int32)
    wavenumber = 0.25 * bin_number.astype(jnp.float32)
    geometry = jnp.take(panel_geom, panel_slot[0], axis=1)
    listeners = jnp.take(observer_pos, observer_slot[0], axis=1)
    scale = 1.0 / math.sqrt(panel_count * lax.axis_size("obs"))
    all_geometry = lax.all_gather(geometry, "obs", axis=1, tiled=True)
    return contribution(
        listeners,
        all_geometry,
        lax.all_gather(spectra, "obs", axis=4, tiled=True),
        wavenumber,
        scale,
    )


def solution(mesh):
    placed = (
        P(None, "freq", "obs"),
        P(None, "obs"),
        P("obs", None),
        P(None, "obs"),
        P("obs", None),
    )
    return jax.shard_map(
        local, mesh=mesh, in_specs=placed, out_specs=P("obs", "freq", None, None), check_vma=False
    )
```

profile of v0, /device:TPU:1, one launch (start us, length us, event | category | flops | bytes accessed | tf_op | source)
XLA Modules:
  0.0 548.8 jit_solution(15049817675653690594)
XLA Ops:
  8.9 23.7 %all_to_all.18 = bf16[2,64,4,1,512]{4,2,0,3,1:T(4,128)(2,1)S(1)} all-to-all(bf16[2,64,4,1,512]{4,2,0,3,1:T(4,128)(2,1)S(1)} %copy.28), channel_id=1, replica_groups=mesh['freq'=16,'obs'=16] {'freq'}, dimensions={1} | all-to-all | bytes 1048576 | tf_op jit(solution)/shard_map/all_to_all | solution.py:83
  35.1 64.4 %all_gather.7 = f32[4,8192]{0,1:T(8,128)} all-gather(f32[4,512]{0,1:T(8,128)S(1)} %select_bitcast_fusion), channel_id=1, replica_groups=mesh['freq'=16,'obs'=16] {'obs'}, dimensions={1}, use_global_device_ids=true | all-gather | bytes 139264 | tf_op jit(solution)/shard_map/all_gather | solution.py:90
  103.5 29.9 %all-gather.3.cloned.1.call-done = bf16[2,4,4,16,1,8192]{5,3,2,1,0,4:T(8,128)(2,1)} async-done(((bf16[2,4,4,16,1,512]{5,3,2,1,0,4:T(8,128)(2,1)}), bf16[2,4,4,16,1,8192]{5,3,2,1,0,4:T(8,128)(2,1)}) %all-gather.3.cloned.1.call-update) | async-done | bytes 8388624 | tf_op jit(solution)/shard_map/all_gather | solution.py:94
  133.4 407.8 %while.14 = (s32[]{:T(128)}, f32[256,4,2,16]{0,3,2,1:T(8,128)S(1)}, s32[16]{0:T(128)S(1)}, bf16[2,4,4,16,8192]{4,3,2,1,0:T(8,128)(2,1)}, f32[3,256]{1,0:T(4,128)...) while((s32[]{:T(128)}, f32[256,4,2,16]{0,3,2,1:T(8,128)S(1)}, ...), condition=%wide.region_3.4_spmd.clone.clone.clone, body=%wide.region_1.3_spmd.clone.clone.clone.sunk | while | flops 303891008 | bytes 49058168 | solution.py:72
  136.3 10.5 %multiply_convert_fusion.9 = (bf16[4,256,1,512]{3,1,2,0:T(8,128)(2,1)S(1)}, bf16[4,256,1,512]{3,1,2,0:T(8,128)(2,1)S(1)}, bf16[4,256,1,512]{3,1,2,0:T(8,128)(2,1...) fusion(f32[256,512]{1,0:T(8,128)S(1)} %get-tuple-element.273, ...), kind=kLoop, calls=%fused_computation.35.clone.1 | loop fusion | flops 15204352 | bytes 11536432 | tf_op jit(solution)/shard_map/convert.11
  154.4 4.5 fusion.51
  161.8 10.5 %multiply_convert_fusion.9 = (bf16[4,256,1,512]{3,1,2,0:T(8,128)(2,1)S(1)}, bf16[4,256,1,512]{3,1,2,0:T(8,128)(2,1)S(1)}, bf16[4,256,1,512]{3,1,2,0:T(8,128)(2,1...) fusion(f32[256,512]{1,0:T(8,128)S(1)} %get-tuple-element.273, ...), kind=kLoop, calls=%fused_computation.35.clone.1 | loop fusion | flops 15204352 | bytes 11536432 | tf_op jit(solution)/shard_map/convert.11
  179.9 4.5 fusion.51
  187.3 10.5 %multiply_convert_fusion.9 = (bf16[4,256,1,512]{3,1,2,0:T(8,128)(2,1)S(1)}, bf16[4,256,1,512]{3,1,2,0:T(8,128)(2,1)S(1)}, bf16[4,256,1,512]{3,1,2,0:T(8,128)(2,1...) fusion(f32[256,512]{1,0:T(8,128)S(1)} %get-tuple-element.273, ...), kind=kLoop, calls=%fused_computation.35.clone.1 | loop fusion | flops 15204352 | bytes 11536432 | tf_op jit(solution)/shard_map/convert.11
  205.4 4.5 fusion.51
  212.8 10.5 %multiply_convert_fusion.9 = (bf16[4,256,1,512]{3,1,2,0:T(8,128)(2,1)S(1)}, bf16[4,256,1,512]{3,1,2,0:T(8,128)(2,1)S(1)}, bf16[4,256,1,512]{3,1,2,0:T(8,128)(2,1...) fusion(f32[256,512]{1,0:T(8,128)S(1)} %get-tuple-element.273, ...), kind=kLoop, calls=%fused_computation.35.clone.1 | loop fusion | flops 15204352 | bytes 11536432 | tf_op jit(solution)/shard_map/convert.11
  230.9 4.5 fusion.51
  238.2 10.5 %multiply_convert_fusion.9 = (bf16[4,256,1,512]{3,1,2,0:T(8,128)(2,1)S(1)}, bf16[4,256,1,512]{3,1,2,0:T(8,128)(2,1)S(1)}, bf16[4,256,1,512]{3,1,2,0:T(8,128)(2,1...) fusion(f32[256,512]{1,0:T(8,128)S(1)} %get-tuple-element.273, ...), kind=kLoop, calls=%fused_computation.35.clone.1 | loop fusion | flops 15204352 | bytes 11536432 | tf_op jit(solution)/shard_map/convert.11
  256.3 4.5 fusion.51
  263.7 10.5 %multiply_convert_fusion.9 = (bf16[4,256,1,512]{3,1,2,0:T(8,128)(2,1)S(1)}, bf16[4,256,1,512]{3,1,2,0:T(8,128)(2,1)S(1)}, bf16[4,256,1,512]{3,1,2,0:T(8,128)(2,1...) fusion(f32[256,512]{1,0:T(8,128)S(1)} %get-tuple-element.273, ...), kind=kLoop, calls=%fused_computation.35.clone.1 | loop fusion | flops 15204352 | bytes 11536432 | tf_op jit(solution)/shard_map/convert.11
  281.8 4.5 fusion.51
  289.2 10.5 %multiply_convert_fusion.9 = (bf16[4,256,1,512]{3,1,2,0:T(8,128)(2,1)S(1)}, bf16[4,256,1,512]{3,1,2,0:T(8,128)(2,1)S(1)}, bf16[4,256,1,512]{3,1,2,0:T(8,128)(2,1...) fusion(f32[256,512]{1,0:T(8,128)S(1)} %get-tuple-element.273, ...), kind=kLoop, calls=%fused_computation.35.clone.1 | loop fusion | flops 15204352 | bytes 11536432 | tf_op jit(solution)/shard_map/convert.11
  307.3 4.5 fusion.51
  314.7 10.5 %multiply_convert_fusion.9 = (bf16[4,256,1,512]{3,1,2,0:T(8,128)(2,1)S(1)}, bf16[4,256,1,512]{3,1,2,0:T(8,128)(2,1)S(1)}, bf16[4,256,1,512]{3,1,2,0:T(8,128)(2,1...) fusion(f32[256,512]{1,0:T(8,128)S(1)} %get-tuple-element.273, ...), kind=kLoop, calls=%fused_computation.35.clone.1 | loop fusion | flops 15204352 | bytes 11536432 | tf_op jit(solution)/shard_map/convert.11
  332.8 4.5 fusion.51
  340.2 10.5 %multiply_convert_fusion.9 = (bf16[4,256,1,512]{3,1,2,0:T(8,128)(2,1)S(1)}, bf16[4,256,1,512]{3,1,2,0:T(8,128)(2,1)S(1)}, bf16[4,256,1,512]{3,1,2,0:T(8,128)(2,1...) fusion(f32[256,512]{1,0:T(8,128)S(1)} %get-tuple-element.273, ...), kind=kLoop, calls=%fused_computation.35.clone.1 | loop fusion | flops 15204352 | bytes 11536432 | tf_op jit(solution)/shard_map/convert.11
  358.3 4.5 fusion.51
  365.7 10.5 %multiply_convert_fusion.9 = (bf16[4,256,1,512]{3,1,2,0:T(8,128)(2,1)S(1)}, bf16[4,256,1,512]{3,1,2,0:T(8,128)(2,1)S(1)}, bf16[4,256,1,512]{3,1,2,0:T(8,128)(2,1...) fusion(f32[256,512]{1,0:T(8,128)S(1)} %get-tuple-element.273, ...), kind=kLoop, calls=%fused_computation.35.clone.1 | loop fusion | flops 15204352 | bytes 11536432 | tf_op jit(solution)/shard_map/convert.11
  383.8 4.5 fusion.51
  391.2 10.5 %multiply_convert_fusion.9 = (bf16[4,256,1,512]{3,1,2,0:T(8,128)(2,1)S(1)}, bf16[4,256,1,512]{3,1,2,0:T(8,128)(2,1)S(1)}, bf16[4,256,1,512]{3,1,2,0:T(8,128)(2,1...) fusion(f32[256,512]{1,0:T(8,128)S(1)} %get-tuple-element.273, ...), kind=kLoop, calls=%fused_computation.35.clone.1 | loop fusion | flops 15204352 | bytes 11536432 | tf_op jit(solution)/shard_map/convert.11
  409.3 4.5 fusion.51
  416.7 10.5 %multiply_convert_fusion.9 = (bf16[4,256,1,512]{3,1,2,0:T(8,128)(2,1)S(1)}, bf16[4,256,1,512]{3,1,2,0:T(8,128)(2,1)S(1)}, bf16[4,256,1,512]{3,1,2,0:T(8,128)(2,1...) fusion(f32[256,512]{1,0:T(8,128)S(1)} %get-tuple-element.273, ...), kind=kLoop, calls=%fused_computation.35.clone.1 | loop fusion | flops 15204352 | bytes 11536432 | tf_op jit(solution)/shard_map/convert.11
  434.8 4.5 fusion.51
  442.2 10.5 %multiply_convert_fusion.9 = (bf16[4,256,1,512]{3,1,2,0:T(8,128)(2,1)S(1)}, bf16[4,256,1,512]{3,1,2,0:T(8,128)(2,1)S(1)}, bf16[4,256,1,512]{3,1,2,0:T(8,128)(2,1...) fusion(f32[256,512]{1,0:T(8,128)S(1)} %get-tuple-element.273, ...), kind=kLoop, calls=%fused_computation.35.clone.1 | loop fusion | flops 15204352 | bytes 11536432 | tf_op jit(solution)/shard_map/convert.11
  467.7 10.5 %multiply_convert_fusion.9 = (bf16[4,256,1,512]{3,1,2,0:T(8,128)(2,1)S(1)}, bf16[4,256,1,512]{3,1,2,0:T(8,128)(2,1)S(1)}, bf16[4,256,1,512]{3,1,2,0:T(8,128)(2,1...) fusion(f32[256,512]{1,0:T(8,128)S(1)} %get-tuple-element.273, ...), kind=kLoop, calls=%fused_computation.35.clone.1 | loop fusion | flops 15204352 | bytes 11536432 | tf_op jit(solution)/shard_map/convert.11
  493.1 10.5 %multiply_convert_fusion.9 = (bf16[4,256,1,512]{3,1,2,0:T(8,128)(2,1)S(1)}, bf16[4,256,1,512]{3,1,2,0:T(8,128)(2,1)S(1)}, bf16[4,256,1,512]{3,1,2,0:T(8,128)(2,1...) fusion(f32[256,512]{1,0:T(8,128)S(1)} %get-tuple-element.273, ...), kind=kLoop, calls=%fused_computation.35.clone.1 | loop fusion | flops 15204352 | bytes 11536432 | tf_op jit(solution)/shard_map/convert.11
  518.6 10.5 %multiply_convert_fusion.9 = (bf16[4,256,1,512]{3,1,2,0:T(8,128)(2,1)S(1)}, bf16[4,256,1,512]{3,1,2,0:T(8,128)(2,1)S(1)}, bf16[4,256,1,512]{3,1,2,0:T(8,128)(2,1...) fusion(f32[256,512]{1,0:T(8,128)S(1)} %get-tuple-element.273, ...), kind=kLoop, calls=%fused_computation.35.clone.1 | loop fusion | flops 15204352 | bytes 11536432 | tf_op jit(solution)/shard_map/convert.11
  (298 shorter events, 184.5 us)
Async XLA Ops:
  6.5 1.6 copy-start
  6.5 126.9 %all-gather.3.cloned.1.call-start = ((), (), s32[]{:S(2)}) async-start(), calls=%async_computation.1 | async-start | bytes 8912896 | tf_op jit(solution)/shard_map/all_gather | solution.py:94
  8.5 25.2 %copy-start.1 = (f32[4,512]{1,0:T(4,128)S(1)}, f32[4,512]{1,0:T(4,128)}, u32[]{:S(2)}) copy-start(f32[4,512]{1,0:T(4,128)} %param.8) | copy-start | bytes 24580
  8.5 25.4 %copy-start.2 = (s32[1,512]{1,0:T(1,128)S(1)}, s32[1,512]{1,0:T(1,128)}, u32[]{:S(2)}) copy-start(s32[1,512]{1,0:T(1,128)} %param.9) | copy-start | bytes 6148
  99.6 2.9 copy-start.3
  99.6 3.0 copy-start.4
  541.2 0.7 copy-start.5
Sparse Core Ops, SparseCore 0:
  33.8 99.5 all-gather.2
where the time goes:
time: 550 us; the launch traced here: 549 us
  other arithmetic  286 us (52%)
  blocking collectives  88.1 us (16%)
  matrix products  72.1 us (13%)
  local copies, waits for them, and re-layouts  47.5 us (9%)
  waiting for transfers between devices  29.9 us (5%)
  between operations  14.3 us (3%)
  loops' own time  10.7 us (2%)
    another operation x17, other arithmetic  168 us
    another operation x64, other arithmetic, green_tile(): return jnp.stack(pieces, 2).astype(jnp.bfloat16)  76.1 us
    dot_general x16, matrix products, add_block(): jnp.einsum('focxp,fzcxgp->ofzg', tile, sides, preferred_element_type=jnp....  71.8 us
    all_gather x1, blocking collectives, local(): all_geometry = lax.all_gather(geometry, 'obs', axis=1, tiled=True)  64.4 us
    all_gather x1, waiting for transfers between devices, local(): lax.all_gather(spectra, 'obs', axis=4, tiled=True)  29.9 us
    all_to_all x1, blocking collectives, local(): lax.all_to_all(spectra, 'freq', split_axis=1, concat_axis=3, tiled=True)  23.7 us
    neg x16, other arithmetic, source_sides(): first = jnp.stack([real_part, -imag_part], 2)  16 us
    squeeze x16, local copies, waits for them, and re-layouts, source_sides(): first = jnp.stack([real_part, -imag_part], 2)  15.6 us
  transfers between devices with their start and end apart: 1, of which 1 were waited for; matrix products, arithmetic and copies ran while one was open for 1% of the time, Pallas kernels for 0%

commit v1 on v0

v1 whole, which is shorter than its diff:
```python
import functools
import math

import jax
import jax.numpy as jnp
import numpy as np
from jax import lax
from jax.experimental import pallas as pl
from jax.experimental.pallas import tpu as pltpu
from jax.sharding import PartitionSpec as P

WIN = 128
FREQS = 64
NF = 16
NO = 16
BINS = 4
PAN = 512
OBS = 256
CH = 4
HOLD = 4
ROWS = 6 * PAN
SUB = 16
F32 = jnp.float32
BF16 = jnp.bfloat16
MESH = pl.DeviceIdType.MESH

SIN_POLY = (4.4428797, -7.3078165, 3.5977743, -0.7911994)
COS_POLY = (1.414204, -6.9776373, 5.715188, -1.7282139)
STEP_POLY = (9.9999994e-01, -3.1249965e-02, 1.6275267e-04, -3.3845342e-07, 3.5696468e-10)


def dft_table():
    steps = np.arange(WIN, dtype=np.int32)
    bins = np.arange(1, FREQS + 1, dtype=np.int32)
    angles = np.float32(2.0 * math.pi / WIN) * (bins[:, None] * steps[None, :] % WIN).astype(np.float32)
    hann = np.float32(0.5) - np.float32(0.5) * np.cos(np.float32(2.0 * math.pi / WIN) * steps.astype(np.float32))
    weighted = hann[None, :] * (np.float32(1.0) / np.sqrt(np.sum(hann * hann)))
    parts = np.stack([np.cos(angles) * weighted, -np.sin(angles) * weighted], 1)
    return parts.reshape(2 * FREQS, WIN).astype(jnp.bfloat16)


def poly(coefs, x):
    total = coefs[-1] * x + coefs[-2]
    for coef in coefs[-3::-1]:
        total = total * x + coef
    return total


def pieces(x):
    first = x.astype(BF16).astype(F32)
    rest = x - first
    second = rest.astype(BF16).astype(F32)
    return first, second, (rest - second).astype(BF16).astype(F32)


def permuted(array, slot):
    n = array.shape[1]
    hot = (lax.broadcasted_iota(jnp.int32, (n, n), 0) == slot).astype(F32).astype(BF16)
    stacked = jnp.concatenate(pieces(array), 0).astype(BF16)
    picked = jnp.dot(stacked, hot, preferred_element_type=F32)
    return picked[0:8] + picked[8:16] + picked[16:24]


def tile_part(d2, kappa):
    inverse = lax.rsqrt(d2)
    distance = d2 * inverse
    turns = distance * kappa
    turns = turns - ((turns + 12582912.0) - 12582912.0)
    square = turns * turns
    sine = turns * poly(SIN_POLY, square)
    cosine = poly(COS_POLY, square)
    amp = inverse * inverse
    scaled = amp * sine
    c1 = amp - scaled * sine
    s1 = scaled * cosine
    step_cos = poly(STEP_POLY, d2)
    rest = 1.0 - step_cos * step_cos
    step_sin = rest * lax.rsqrt(rest)
    cc, ss, sc, cs = c1 * step_cos, s1 * step_sin, s1 * step_cos, c1 * step_sin
    c0, c2 = cc + ss, cc - ss
    s0, s2 = sc - cs, sc + cs
    twice = step_cos + step_cos
    c3 = twice * c2 - c1
    s3 = twice * s2 - s1
    return ((c0, s0), (c1, s1), (c2, s2), (c3, s3)), inverse, distance


def generate(store, k, quarter, d2_ref, parity, kappa):
    def one(sub, carry):
        base = pl.multiple_of(quarter * 128 + sub * SUB, SUB)
        d2 = d2_ref[parity, pl.ds(pl.multiple_of(sub * SUB, SUB), SUB), :]
        factors, inverse, distance = tile_part(d2, kappa)
        inverse, distance = inverse.astype(BF16), distance.astype(BF16)
        for f in range(BINS):
            c, s = factors[f][0].astype(BF16), factors[f][1].astype(BF16)
            for at, part in enumerate((c, s, c * inverse, s * inverse, c * distance, s * distance)):
                store[k, f, pl.ds(pl.multiple_of(base + at * PAN, SUB), SUB), :] = part
        return carry

    lax.fori_loop(0, 128 // SUB, one, 0, unroll=True)


def contract(store, k, f, le_ref, lm_ref, place_ref, block):
    out = jnp.dot(le_ref[f], store[k, f, 0 : 4 * PAN, :], preferred_element_type=F32)
    mono = jnp.dot(lm_ref[f], store[k, f, 4 * PAN : 6 * PAN, :], preferred_element_type=F32)
    place = place_ref[block]
    return (
        out[0:32] * place[0:1]
        + out[32:64] * place[1:2]
        + out[64:96] * place[2:3]
        + (out[96:128] + mono)
    )


def kernel(
    table_ref,
    samples_ref,
    geom_ref,
    slot_ref,
    pos_ref,
    pos_slot_ref,
    out_ref,
    eight,
    geometry,
    left,
    place_in,
    right,
    d2_ref,
    spec_out,
    spec_in,
    perm,
    le_ref,
    lm_ref,
    store_a,
    store_b,
    part_out,
    part_in,
    place_send,
    place_recv,
    spec_send,
    spec_recv,
    part_send,
    part_recv,
):
    q = lax.axis_index("freq")
    me = lax.axis_index("obs")

    barrier = pltpu.get_barrier_semaphore()

    def greet(step, carry):
        pl.semaphore_signal(barrier, inc=1, device_id=(q, lax.rem(me + step, NO)), device_id_type=MESH)
        pl.semaphore_signal(barrier, inc=1, device_id=(lax.rem(q + step, NF), me), device_id_type=MESH)
        return carry

    lax.fori_loop(1, NO, greet, 0)

    eight[...] = jnp.zeros_like(eight)
    eight[0:3, 0:OBS] = pos_ref[...]
    seen = permuted(eight[:, 0:OBS], pos_slot_ref[...])
    place_in[0] = seen
    place_in[0, 3:4, :] = seen[0:1] * seen[0:1] + seen[1:2] * seen[1:2] + seen[2:3] * seen[2:3]
    place_in[0, 4:5, :] = jnp.ones((1, OBS), F32)

    pl.semaphore_wait(barrier, NO - 1 + NF - 1)

    def place_copy(step):
        return pltpu.make_async_remote_copy(
            src_ref=place_in.at[0],
            dst_ref=place_in.at[NO - step],
            send_sem=place_send.at[step],
            recv_sem=place_recv.at[NO - step],
            device_id=(q, lax.rem(me + step, NO)),
            device_id_type=MESH,
        )

    def spec_copy(step):
        owner = lax.rem(q + step, NF)
        return pltpu.make_async_remote_copy(
            src_ref=spec_out.at[owner],
            dst_ref=spec_in.at[q],
            send_sem=spec_send.at[step],
            recv_sem=spec_recv.at[NF - step],
            device_id=(owner, me),
            device_id_type=MESH,
        )

    def part_copy(step):
        return pltpu.make_async_remote_copy(
            src_ref=part_out.at[step],
            dst_ref=part_in.at[NO - step],
            send_sem=part_send.at[step],
            recv_sem=part_recv.at[NO - step],
            device_id=(q, lax.rem(me + step, NO)),
            device_id_type=MESH,
        )

    def start_all(copy):
        def one(step, carry):
            copy(step).start()
            return carry

        lax.fori_loop(1, NO, one, 0)

    start_all(place_copy)

    for c in range(0, CH, 2):
        pair = [
            jnp.dot(table_ref[...], samples_ref[c + d], preferred_element_type=F32).reshape(NF, 2 * BINS, PAN)
            for d in range(2)
        ]
        spec_out[:, c * 8 : c * 8 + 16, :] = jnp.concatenate(pair, 1).astype(BF16)
    start_all(spec_copy)
    spec_in[q] = spec_out[q]

    eight[...] = jnp.zeros_like(eight)
    eight[0:4, :] = geom_ref[...]
    geometry[...] = permuted(eight[...], slot_ref[...])
    geo = geometry[...]
    eight[0:3, :] = -2.0 * geo[0:3]
    eight[3:4, :] = jnp.ones((1, PAN), F32)
    eight[4:5, :] = geo[0:1] * geo[0:1] + geo[1:2] * geo[1:2] + geo[2:3] * geo[2:3]
    one, two, three = pieces(eight[...])
    side = jnp.concatenate([one, two, one, three, two, one, jnp.zeros((80, PAN), F32)], 0)
    left[...] = side.T.astype(BF16)

    def spread(block):
        one, two, three = pieces(place_in[block])
        right[block] = jnp.concatenate([one, one, two, one, two, three, jnp.zeros((80, OBS), F32)], 0).astype(BF16)

    def distances(turn):
        block, quarter = turn // 4, lax.rem(turn, 4)
        d2_ref[lax.rem(turn, 2)] = jnp.dot(
            left[pl.ds(pl.multiple_of(quarter * 128, 128), 128), :], right[block], preferred_element_type=F32
        )

    kappa = (q.astype(F32) + 0.5) * (0.5 / math.pi)

    def run(gen_store, gen_first, mm_store, mm_first, count):
        def block_step(k, carry):
            def quarter_step(h, inner):
                if mm_store is not None:
                    block = mm_first + k
                    result = contract(mm_store, k, h, le_ref, lm_ref, place_in, block)
                    part_out[block, pl.ds(pl.multiple_of(h * 32, 32), 32), :] = result.astype(BF16)
                if gen_store is not None:
                    turn = (gen_first + k) * 4 + h
                    generate(gen_store, k, h, d2_ref, lax.rem(turn, 2), kappa)
                    distances(jnp.minimum(turn + 1, 4 * NO - 1))
                return inner

            lax.fori_loop(0, 4, quarter_step, 0)
            if mm_store is not None:
                block = mm_first + k

                @pl.when(block > 0)
                def _():
                    part_copy(block).start()

            return carry

        lax.fori_loop(0, count, block_step, 0)

    spread(0)
    distances(jnp.int32(0))

    row = lax.broadcasted_iota(jnp.int32, (PAN, PAN), 0)
    col = lax.broadcasted_iota(jnp.int32, (PAN, PAN), 1)
    source = (row & 15) * 32 + ((row >> 5) & 3) * 8 + (row >> 7) * 2 + ((row >> 4) & 1)
    perm[...] = (source == col).astype(F32).astype(BF16)

    def await_place(step, carry):
        place_copy(step).wait_send()
        place_copy(NO - step).wait_recv()
        spread(step)
        return carry

    lax.fori_loop(1, NO, await_place, 0)
    run(store_a, 0, None, 0, HOLD)

    def await_spec(step, carry):
        spec_copy(step).wait_send()
        spec_copy(NF - step).wait_recv()
        return carry

    lax.fori_loop(1, NF, await_spec, 0)

    geo = geometry[...]
    weight = geo[3:4] * (0.25 / math.pi / math.sqrt(PAN * NO))
    everything = spec_in[...].reshape(PAN, PAN)
    for f in range(BINS):
        wave = (q * BINS + (f + 1)).astype(F32) * 0.25
        rows = jnp.dot(perm[f * 128 : f * 128 + 128, :], everything, preferred_element_type=F32) * weight
        mono, load = rows[0:32], [rows[32 * j + 32 : 32 * j + 64] for j in range(3)]
        load.append(-(load[0] * geo[0:1] + load[1] * geo[1:2] + load[2] * geo[2:3]))
        plain = jnp.concatenate(load, 0)
        turned = jnp.concatenate([x for part in load for x in (-part[16:32], part[0:16])], 0)
        mono_turned = jnp.concatenate([-mono[16:32], mono[0:16]], 0)
        le_ref[f, :, 0:PAN] = (turned * wave).astype(BF16)
        le_ref[f, :, PAN : 2 * PAN] = (plain * wave).astype(BF16)
        le_ref[f, :, 2 * PAN : 3 * PAN] = plain.astype(BF16)
        le_ref[f, :, 3 * PAN : 4 * PAN] = (-turned).astype(BF16)
        lm_ref[f, :, 0:PAN] = (mono_turned * -wave).astype(BF16)
        lm_ref[f, :, PAN : 2 * PAN] = (mono * -wave).astype(BF16)

    rounds = NO // HOLD

    def both(t, carry):
        run(store_b, (2 * t + 1) * HOLD, store_a, 2 * t * HOLD, HOLD)
        run(store_a, (2 * t + 2) * HOLD, store_b, (2 * t + 1) * HOLD, HOLD)
        return carry

    lax.fori_loop(0, rounds // 2 - 1, both, 0)
    run(store_b, (rounds - 1) * HOLD, store_a, (rounds - 2) * HOLD, HOLD)
    run(None, 0, store_b, (rounds - 1) * HOLD, HOLD)

    out_ref[...] = part_out[0].astype(F32)

    def finish(step, carry):
        part_copy(step).wait_send()
        part_copy(NO - step).wait_recv()
        out_ref[...] += part_in[step].astype(F32)
        return carry

    lax.fori_loop(1, NO, finish, 0)


def local(samples, panel_geom, panel_slot, observer_pos, observer_slot):
    vmem = pl.BlockSpec(memory_space=pltpu.VMEM)
    dma = pltpu.SemaphoreType.DMA
    out = pl.pallas_call(
        kernel,
        out_shape=jax.ShapeDtypeStruct((BINS * 2 * NF, OBS), F32),
        in_specs=[vmem] * 6,
        out_specs=vmem,
        scratch_shapes=[
            pltpu.VMEM((8, PAN), F32),
            pltpu.VMEM((8, PAN), F32),
            pltpu.VMEM((PAN, 128), BF16),
            pltpu.VMEM((NO, 8, OBS), F32),
            pltpu.VMEM((NO, 128, OBS), BF16),
            pltpu.VMEM((2, 128, OBS), F32),
            pltpu.VMEM((NF, 32, PAN), BF16),
            pltpu.VMEM((NF, 32, PAN), BF16),
            pltpu.VMEM((PAN, PAN), BF16),
            pltpu.VMEM((BINS, 128, 4 * PAN), BF16),
            pltpu.VMEM((BINS, 32, 2 * PAN), BF16),
            pltpu.VMEM((HOLD, BINS, ROWS, OBS), BF16),
            pltpu.VMEM((HOLD, BINS, ROWS, OBS), BF16),
            pltpu.VMEM((NO, 128, OBS), BF16),
            pltpu.VMEM((NO, 128, OBS), BF16),
            dma((NO,)),
            dma((NO,)),
            dma((NF,)),
            dma((NF,)),
            dma((NO,)),
            dma((NO,)),
        ],
        compiler_params=pltpu.CompilerParams(
            collective_id=0, has_side_effects=True, vmem_limit_bytes=60 * 2**20
        ),
    )(jnp.asarray(dft_table()), samples, panel_geom, panel_slot, observer_pos, observer_slot)
    return out.reshape(BINS, 2, NF, OBS).transpose(3, 0, 1, 2)


def solution(mesh):
    placed = (
        P(None, "freq", "obs"),
        P(None, "obs"),
        P("obs", None),
        P(None, "obs"),
        P("obs", None),
    )
    return jax.shard_map(
        local, mesh=mesh, in_specs=placed, out_specs=P("obs", "freq", None, None), check_vma=False
    )
```

time: 550 us -> 66.2 us (0.12)
  other arithmetic: 286 us -> 0 us
  blocking collectives: 88.1 us -> 0 us
  matrix products: 72.1 us -> 0 us
  Pallas kernels: 0 us -> 64.2 us
  local copies, waits for them, and re-layouts: 47.5 us -> 1.57 us
  waiting for transfers between devices: 29.9 us -> 0 us
  between operations: 14.3 us -> 0.01 us
  loops' own time: 10.7 us -> 0 us
    another operation x97 -> x0, other arithmetic: 258 us -> none
    dot_general x17 -> x0, matrix products: 72.1 us -> none  [the longest x16 71.8 us: add_block(): jnp.einsum('focxp,fzcxgp->ofzg', tile, sides, preferred_element_type=jnp....]
    all_gather x1 -> x0, blocking collectives: 64.4 us -> none  [local(): all_geometry = lax.all_gather(geometry, 'obs', axis=1, tiled=True)]
    pallas_call x0 -> x1, Pallas kernels: none -> 64.2 us  [local(): pl.pallas_call(kernel, out_shape=jax.ShapeDtypeStruct((BINS * 2 * NF, OBS...]
    all_gather x1 -> x0, waiting for transfers between devices: 29.9 us -> none  [local(): lax.all_gather(spectra, 'obs', axis=4, tiled=True)]
    all_to_all x1 -> x0, blocking collectives: 23.7 us -> none  [local(): lax.all_to_all(spectra, 'freq', split_axis=1, concat_axis=3, tiled=True)]
    neg x16 -> x0, other arithmetic: 16 us -> none  [source_sides(): first = jnp.stack([real_part, -imag_part], 2)]
    squeeze x16 -> x0, local copies, waits for them, and re-layouts: 15.6 us -> none  [source_sides(): first = jnp.stack([real_part, -imag_part], 2)]
  transfers between devices with their start and end apart: 1 -> 0, of which waited for: 1 -> 0; matrix products, arithmetic and copies ran while one was open for 1% -> 0% of each run, Pallas kernels for 0% -> 0%
where the time goes in v1:
time: 66.2 us; the launch traced here: 65.8 us
  Pallas kernels  64.2 us (97%)
  local copies, waits for them, and re-layouts  1.57 us (2%)
    pallas_call x1, Pallas kernels, local(): pl.pallas_call(kernel, out_shape=jax.ShapeDtypeStruct((BINS * 2 * NF, OBS...  64.2 us
    unnamed x1, local copies, waits for them, and re-layouts  1.57 us

profile of v1, /device:TPU:1, one launch (start us, length us, event | category | flops | bytes accessed | tf_op | source)
XLA Modules:
  0.0 65.8 jit_solution(16916534152732766658)
XLA Ops:
  0.0 64.2 %shard_map.64 = f32[128,256]{1,0:T(8,128)} custom-call(bf16[128,128]{1,0:T(8,128)(2,1)} %constant.2.clone.table_ref, bf16[4,128,512]{2,1,0:T(8,128)(2,1)} %samples_ref.1, f32[4,512]{1,0:T(4,128)} %geom_ref.1, s32[1,512]{1,0:T(1,128)} %slot_ref.1, f32[3,256]{1,0:T(4,128)} %pos_ref.1, s32[1,256]{1,0:T(1,128)} %pos_slot_ref.1), custom_call_target="tpu_custom_call" | custom-call | tf_op jit(solution)/shard_map/pallas_call | solution.py:330
  64.2 1.6 %copy.8 = f32[256,4,2,16]{0,3,2,1:T(8,128)} copy(f32[256,4,2,16]{0,3,2,1:T(8,128)} %bitcast.3) | data formatting | bytes 262144

commit v2 on v1

--- a/solution.py
+++ b/solution.py
@@ -17,8 +17,9 @@
 PAN = 512
 OBS = 256
 CH = 4
-HOLD = 4
-ROWS = 6 * PAN
+HELD = 8
+ROWS = 4 * PAN
+GROUPS = 160
 SUB = 16
 F32 = jnp.float32
 BF16 = jnp.bfloat16
@@ -26,7 +27,7 @@
 
 SIN_POLY = (4.4428797, -7.3078165, 3.5977743, -0.7911994)
 COS_POLY = (1.414204, -6.9776373, 5.715188, -1.7282139)
-STEP_POLY = (9.9999994e-01, -3.1249965e-02, 1.6275267e-04, -3.3845342e-07, 3.5696468e-10)
+STEP_POLY = (9.9999505e-01, -3.1246377e-02, 1.6224394e-04, -3.1450108e-07)
 
 
 def dft_table():
@@ -61,10 +62,13 @@
     return picked[0:8] + picked[8:16] + picked[16:24]
 
 
-def tile_part(d2, kappa):
+def norm(rows):
+    return rows[0:1] * rows[0:1] + rows[1:2] * rows[1:2] + rows[2:3] * rows[2:3]
+
+
+def tile_part(d2, step_poly):
     inverse = lax.rsqrt(d2)
-    distance = d2 * inverse
-    turns = distance * kappa
+    turns = d2 * inverse
     turns = turns - ((turns + 12582912.0) - 12582912.0)
     square = turns * turns
     sine = turns * poly(SIN_POLY, square)
@@ -73,7 +77,7 @@
     scaled = amp * sine
     c1 = amp - scaled * sine
     s1 = scaled * cosine
-    step_cos = poly(STEP_POLY, d2)
+    step_cos = poly(step_poly, d2)
     rest = 1.0 - step_cos * step_cos
     step_sin = rest * lax.rsqrt(rest)
     cc, ss, sc, cs = c1 * step_cos, s1 * step_sin, s1 * step_cos, c1 * step_sin
@@ -82,33 +86,32 @@
     twice = step_cos + step_cos
     c3 = twice * c2 - c1
     s3 = twice * s2 - s1
-    return ((c0, s0), (c1, s1), (c2, s2), (c3, s3)), inverse, distance
-
-
-def generate(store, k, quarter, d2_ref, parity, kappa):
+    return ((c0, s0), (c1, s1), (c2, s2), (c3, s3)), inverse
+
+
+def generate(store, k, quarter, d2_ref, step_poly):
     def one(sub, carry):
         base = pl.multiple_of(quarter * 128 + sub * SUB, SUB)
-        d2 = d2_ref[parity, pl.ds(pl.multiple_of(sub * SUB, SUB), SUB), :]
-        factors, inverse, distance = tile_part(d2, kappa)
-        inverse, distance = inverse.astype(BF16), distance.astype(BF16)
+        d2 = d2_ref[pl.ds(pl.multiple_of(sub * SUB, SUB), SUB), :]
+        factors, inverse = tile_part(d2, step_poly)
         for f in range(BINS):
-            c, s = factors[f][0].astype(BF16), factors[f][1].astype(BF16)
-            for at, part in enumerate((c, s, c * inverse, s * inverse, c * distance, s * distance)):
-                store[k, f, pl.ds(pl.multiple_of(base + at * PAN, SUB), SUB), :] = part
+            c, s = factors[f]
+            for at, part in enumerate((c, s, c * inverse, s * inverse)):
+                store[k, f, pl.ds(pl.multiple_of(base + at * PAN, SUB), SUB), :] = part.astype(BF16)
         return carry
 
     lax.fori_loop(0, 128 // SUB, one, 0, unroll=True)
 
 
-def contract(store, k, f, le_ref, lm_ref, place_ref, block):
-    out = jnp.dot(le_ref[f], store[k, f, 0 : 4 * PAN, :], preferred_element_type=F32)
-    mono = jnp.dot(lm_ref[f], store[k, f, 4 * PAN : 6 * PAN, :], preferred_element_type=F32)
+def contract(store, k, f, rhs_ref, place_ref, block):
+    out = jnp.dot(rhs_ref[f], store[k, f], preferred_element_type=F32)
     place = place_ref[block]
     return (
         out[0:32] * place[0:1]
         + out[32:64] * place[1:2]
         + out[64:96] * place[2:3]
-        + (out[96:128] + mono)
+        + out[96:128]
+        + out[128:160] * place[3:4]
     )
 
 
@@ -124,13 +127,14 @@
     geometry,
     left,
     place_in,
+    place,
     right,
-    d2_ref,
+    d2_a,
+    d2_b,
     spec_out,
     spec_in,
     perm,
-    le_ref,
-    lm_ref,
+    rhs_ref,
     store_a,
     store_b,
     part_out,
@@ -158,8 +162,6 @@
     eight[0:3, 0:OBS] = pos_ref[...]
     seen = permuted(eight[:, 0:OBS], pos_slot_ref[...])
     place_in[0] = seen
-    place_in[0, 3:4, :] = seen[0:1] * seen[0:1] + seen[1:2] * seen[1:2] + seen[2:3] * seen[2:3]
-    place_in[0, 4:5, :] = jnp.ones((1, OBS), F32)
 
     pl.semaphore_wait(barrier, NO - 1 + NF - 1)
 
@@ -215,53 +217,68 @@
     eight[...] = jnp.zeros_like(eight)
     eight[0:4, :] = geom_ref[...]
     geometry[...] = permuted(eight[...], slot_ref[...])
+    kappa = (q.astype(F32) + 0.5) * (0.5 / math.pi)
+    scale = jnp.full((8, 1), kappa, F32)
+    middle = jnp.sum(geometry[...], 1, keepdims=True) * (1.0 / PAN)
+    geometry[0:3, :] = (geometry[0:3, :] - middle[0:3]) * scale[0:3]
     geo = geometry[...]
     eight[0:3, :] = -2.0 * geo[0:3]
     eight[3:4, :] = jnp.ones((1, PAN), F32)
-    eight[4:5, :] = geo[0:1] * geo[0:1] + geo[1:2] * geo[1:2] + geo[2:3] * geo[2:3]
+    eight[4:5, :] = norm(geo)
     one, two, three = pieces(eight[...])
     side = jnp.concatenate([one, two, one, three, two, one, jnp.zeros((80, PAN), F32)], 0)
     left[...] = side.T.astype(BF16)
 
     def spread(block):
-        one, two, three = pieces(place_in[block])
+        seen = (place_in[block] - middle) * scale
+        place[block] = seen
+        place[block, 3:4, :] = norm(seen)
+        place[block, 4:5, :] = jnp.ones((1, OBS), F32)
+        one, two, three = pieces(place[block])
         right[block] = jnp.concatenate([one, one, two, one, two, three, jnp.zeros((80, OBS), F32)], 0).astype(BF16)
 
-    def distances(turn):
-        block, quarter = turn // 4, lax.rem(turn, 4)
-        d2_ref[lax.rem(turn, 2)] = jnp.dot(
+    def block_at(turn):
+        return lax.rem(turn + 1, NO)
+
+    def distances(turn, d2_ref):
+        block, quarter = block_at(turn // 4), lax.rem(turn, 4)
+        d2_ref[...] = jnp.dot(
             left[pl.ds(pl.multiple_of(quarter * 128, 128), 128), :], right[block], preferred_element_type=F32
         )
 
-    kappa = (q.astype(F32) + 0.5) * (0.5 / math.pi)
-
-    def run(gen_store, gen_first, mm_store, mm_first, count):
+    inverse_square = 1.0 / (kappa * kappa)
+    step_poly = [jnp.float32(STEP_POLY[0])]
+    power = jnp.float32(1.0)
+    for coef in STEP_POLY[1:]:
+        power = power * inverse_square
+        step_poly.append(coef * power)
+
+    def run(count, gen_store=None, gen_slot=0, gen_turn=0, mm_store=None, mm_turn=0, mm_count=1):
         def block_step(k, carry):
-            def quarter_step(h, inner):
-                if mm_store is not None:
-                    block = mm_first + k
-                    result = contract(mm_store, k, h, le_ref, lm_ref, place_in, block)
-                    part_out[block, pl.ds(pl.multiple_of(h * 32, 32), 32), :] = result.astype(BF16)
-                if gen_store is not None:
-                    turn = (gen_first + k) * 4 + h
-                    generate(gen_store, k, h, d2_ref, lax.rem(turn, 2), kappa)
-                    distances(jnp.minimum(turn + 1, 4 * NO - 1))
+            def half_step(half, inner):
+                for h in range(2):
+                    f = half * 2 + h
+                    if mm_store is not None:
+                        for m in range(mm_count):
+                            slot = k * mm_count + m
+                            block = block_at(mm_turn + slot)
+                            result = contract(mm_store, slot, f, rhs_ref, place, block)
+                            part_out[block, pl.ds(pl.multiple_of(f * 32, 32), 32), :] = result.astype(BF16)
+                    if gen_store is not None:
+                        turn = (gen_turn + k) * 4 + f
+                        distances(jnp.minimum(turn + 1, 4 * NO - 1), (d2_b, d2_a)[h])
+                        generate(gen_store, gen_slot + k, f, (d2_a, d2_b)[h], step_poly)
                 return inner
 
-            lax.fori_loop(0, 4, quarter_step, 0)
-            if mm_store is not None:
-                block = mm_first + k
-
-                @pl.when(block > 0)
-                def _():
-                    part_copy(block).start()
-
+            lax.fori_loop(0, 2, half_step, 0)
+            if mm_store is not None and mm_turn < NO - 1:
+                for m in range(mm_count):
+                    part_copy(block_at(mm_turn + k * mm_count + m)).start()
             return carry
 
         lax.fori_loop(0, count, block_step, 0)
 
     spread(0)
-    distances(jnp.int32(0))
 
     row = lax.broadcasted_iota(jnp.int32, (PAN, PAN), 0)
     col = lax.broadcasted_iota(jnp.int32, (PAN, PAN), 1)
@@ -275,7 +292,8 @@
         return carry
 
     lax.fori_loop(1, NO, await_place, 0)
-    run(store_a, 0, None, 0, HOLD)
+    distances(jnp.int32(0), d2_a)
+    run(HELD, store_a)
 
     def await_spec(step, carry):
         spec_copy(step).wait_send()
@@ -284,34 +302,32 @@
 
     lax.fori_loop(1, NF, await_spec, 0)
 
+    def turned(x):
+        return jnp.concatenate([-x[16:32], x[0:16]], 0)
+
     geo = geometry[...]
-    weight = geo[3:4] * (0.25 / math.pi / math.sqrt(PAN * NO))
+    weight = geo[3:4] * (0.25 / math.pi / math.sqrt(PAN * NO)) * (kappa * kappa)
+    square = norm(geo)
     everything = spec_in[...].reshape(PAN, PAN)
     for f in range(BINS):
-        wave = (q * BINS + (f + 1)).astype(F32) * 0.25
+        wave = (q * BINS + (f + 1)).astype(F32) * 0.25 / kappa
         rows = jnp.dot(perm[f * 128 : f * 128 + 128, :], everything, preferred_element_type=F32) * weight
-        mono, load = rows[0:32], [rows[32 * j + 32 : 32 * j + 64] for j in range(3)]
+        mono = turned(rows[0:32]) * wave
+        load = [rows[32 * j + 32 : 32 * j + 64] for j in range(3)]
         load.append(-(load[0] * geo[0:1] + load[1] * geo[1:2] + load[2] * geo[2:3]))
-        plain = jnp.concatenate(load, 0)
-        turned = jnp.concatenate([x for part in load for x in (-part[16:32], part[0:16])], 0)
-        mono_turned = jnp.concatenate([-mono[16:32], mono[0:16]], 0)
-        le_ref[f, :, 0:PAN] = (turned * wave).astype(BF16)
-        le_ref[f, :, PAN : 2 * PAN] = (plain * wave).astype(BF16)
-        le_ref[f, :, 2 * PAN : 3 * PAN] = plain.astype(BF16)
-        le_ref[f, :, 3 * PAN : 4 * PAN] = (-turned).astype(BF16)
-        lm_ref[f, :, 0:PAN] = (mono_turned * -wave).astype(BF16)
-        lm_ref[f, :, PAN : 2 * PAN] = (mono * -wave).astype(BF16)
-
-    rounds = NO // HOLD
-
-    def both(t, carry):
-        run(store_b, (2 * t + 1) * HOLD, store_a, 2 * t * HOLD, HOLD)
-        run(store_a, (2 * t + 2) * HOLD, store_b, (2 * t + 1) * HOLD, HOLD)
-        return carry
-
-    lax.fori_loop(0, rounds // 2 - 1, both, 0)
-    run(store_b, (rounds - 1) * HOLD, store_a, (rounds - 2) * HOLD, HOLD)
-    run(None, 0, store_b, (rounds - 1) * HOLD, HOLD)
+        near = [load[j] + mono * (2.0 * geo[j : j + 1]) for j in range(3)] + [load[3] - mono * square, -mono]
+        far = [turned(x) * wave for x in load] + [jnp.zeros((32, PAN), F32)]
+        for at, side in enumerate((far, near)):
+            rhs_ref[f, :, 2 * at * PAN : (2 * at + 1) * PAN] = jnp.concatenate(side, 0).astype(BF16)
+            rhs_ref[f, :, (2 * at + 1) * PAN : (2 * at + 2) * PAN] = jnp.concatenate(
+                [-turned(x) for x in side], 0
+            ).astype(BF16)
+
+    run(4, store_b, 0, 8, store_a, 0, 2)
+    run(2, store_a, 0, 12, store_b, 8, 2)
+    run(1, store_b, 0, 14, store_a, 12, 2)
+    run(1, store_a, 0, 15, store_b, 14, 1)
+    run(1, mm_store=store_a, mm_turn=15)
 
     out_ref[...] = part_out[0].astype(F32)
 
@@ -337,15 +353,16 @@
             pltpu.VMEM((8, PAN), F32),
             pltpu.VMEM((PAN, 128), BF16),
             pltpu.VMEM((NO, 8, OBS), F32),
+            pltpu.VMEM((NO, 8, OBS), F32),
             pltpu.VMEM((NO, 128, OBS), BF16),
-            pltpu.VMEM((2, 128, OBS), F32),
+            pltpu.VMEM((128, OBS), F32),
+            pltpu.VMEM((128, OBS), F32),
             pltpu.VMEM((NF, 32, PAN), BF16),
             pltpu.VMEM((NF, 32, PAN), BF16),
             pltpu.VMEM((PAN, PAN), BF16),
-            pltpu.VMEM((BINS, 128, 4 * PAN), BF16),
-            pltpu.VMEM((BINS, 32, 2 * PAN), BF16),
-            pltpu.VMEM((HOLD, BINS, ROWS, OBS), BF16),
-            pltpu.VMEM((HOLD, BINS, ROWS, OBS), BF16),
+            pltpu.VMEM((BINS, GROUPS, ROWS), BF16),
+            pltpu.VMEM((HELD, BINS, ROWS, OBS), BF16),
+            pltpu.VMEM((HELD // 2, BINS, ROWS, OBS), BF16),
             pltpu.VMEM((NO, 128, OBS), BF16),
             pltpu.VMEM((NO, 128, OBS), BF16),
             dma((NO,)),

time: 66.2 us -> 59.3 us (0.90)
  Pallas kernels: 64.2 us -> 57.4 us
    pallas_call x1, Pallas kernels: 64.2 us -> 57.4 us  [local(): pl.pallas_call(kernel, out_shape=jax.ShapeDtypeStruct((BINS * 2 * NF, OBS...]
where the time goes in v2:
time: 59.3 us; the launch traced here: 59 us
  Pallas kernels  57.4 us (97%)
  local copies, waits for them, and re-layouts  1.57 us (3%)
    pallas_call x1, Pallas kernels, local(): pl.pallas_call(kernel, out_shape=jax.ShapeDtypeStruct((BINS * 2 * NF, OBS...  57.4 us
    unnamed x1, local copies, waits for them, and re-layouts  1.57 us

profile of v2, /device:TPU:1, one launch (start us, length us, event | category | flops | bytes accessed | tf_op | source)
XLA Modules:
  0.0 59.0 jit_solution(9975104355352899710)
XLA Ops:
  0.0 57.4 %shard_map.64 = f32[128,256]{1,0:T(8,128)} custom-call(bf16[128,128]{1,0:T(8,128)(2,1)} %constant.2.clone.table_ref, bf16[4,128,512]{2,1,0:T(8,128)(2,1)} %samples_ref.1, f32[4,512]{1,0:T(4,128)} %geom_ref.1, s32[1,512]{1,0:T(1,128)} %slot_ref.1, f32[3,256]{1,0:T(4,128)} %pos_ref.1, s32[1,256]{1,0:T(1,128)} %pos_slot_ref.1), custom_call_target="tpu_custom_call" | custom-call | tf_op jit(solution)/shard_map/pallas_call | solution.py:346
  57.4 1.6 %copy.8 = f32[256,4,2,16]{0,3,2,1:T(8,128)} copy(f32[256,4,2,16]{0,3,2,1:T(8,128)} %bitcast.3) | data formatting | bytes 262144

commit v3 on v2

--- a/solution.py
+++ b/solution.py
@@ -133,7 +133,6 @@
     d2_b,
     spec_out,
     spec_in,
-    perm,
     rhs_ref,
     store_a,
     store_b,
@@ -163,8 +162,6 @@
     seen = permuted(eight[:, 0:OBS], pos_slot_ref[...])
     place_in[0] = seen
 
-    pl.semaphore_wait(barrier, NO - 1 + NF - 1)
-
     def place_copy(step):
         return pltpu.make_async_remote_copy(
             src_ref=place_in.at[0],
@@ -203,15 +200,12 @@
 
         lax.fori_loop(1, NO, one, 0)
 
-    start_all(place_copy)
-
     for c in range(0, CH, 2):
         pair = [
             jnp.dot(table_ref[...], samples_ref[c + d], preferred_element_type=F32).reshape(NF, 2 * BINS, PAN)
             for d in range(2)
         ]
         spec_out[:, c * 8 : c * 8 + 16, :] = jnp.concatenate(pair, 1).astype(BF16)
-    start_all(spec_copy)
     spec_in[q] = spec_out[q]
 
     eight[...] = jnp.zeros_like(eight)
@@ -235,15 +229,12 @@
         place[block, 3:4, :] = norm(seen)
         place[block, 4:5, :] = jnp.ones((1, OBS), F32)
         one, two, three = pieces(place[block])
-        right[block] = jnp.concatenate([one, one, two, one, two, three, jnp.zeros((80, OBS), F32)], 0).astype(BF16)
-
-    def block_at(turn):
-        return lax.rem(turn + 1, NO)
+        right[block] = jnp.concatenate([one, one, two, one, two, three, jnp.zeros((16, OBS), F32)], 0).astype(BF16)
 
     def distances(turn, d2_ref):
-        block, quarter = block_at(turn // 4), lax.rem(turn, 4)
+        block, quarter = turn // 4, lax.rem(turn, 4)
         d2_ref[...] = jnp.dot(
-            left[pl.ds(pl.multiple_of(quarter * 128, 128), 128), :], right[block], preferred_element_type=F32
+            left[pl.ds(pl.multiple_of(quarter * 128, 128), 128), 0:64], right[block], preferred_element_type=F32
         )
 
     inverse_square = 1.0 / (kappa * kappa)
@@ -253,27 +244,35 @@
         power = power * inverse_square
         step_poly.append(coef * power)
 
-    def run(count, gen_store=None, gen_slot=0, gen_turn=0, mm_store=None, mm_turn=0, mm_count=1):
+    def await_place(block):
+        place_copy(NO - block).wait_recv()
+        spread(block)
+
+    def run(count, gen_store=None, gen_slot=0, gen_block=0, mm_store=None, mm_slot=0, mm_block=0, mm_count=1):
         def block_step(k, carry):
             def half_step(half, inner):
+                if mm_store is None and gen_block > 0:
+                    @pl.when(half == 1)
+                    def _():
+                        await_place(gen_block + k + 1)
+
                 for h in range(2):
                     f = half * 2 + h
                     if mm_store is not None:
                         for m in range(mm_count):
-                            slot = k * mm_count + m
-                            block = block_at(mm_turn + slot)
-                            result = contract(mm_store, slot, f, rhs_ref, place, block)
-                            part_out[block, pl.ds(pl.multiple_of(f * 32, 32), 32), :] = result.astype(BF16)
+                            at = k * mm_count + m
+                            result = contract(mm_store, mm_slot + at, f, rhs_ref, place, mm_block + at)
+                            part_out[mm_block + at, pl.ds(pl.multiple_of(f * 32, 32), 32), :] = result.astype(BF16)
                     if gen_store is not None:
-                        turn = (gen_turn + k) * 4 + f
-                        distances(jnp.minimum(turn + 1, 4 * NO - 1), (d2_b, d2_a)[h])
+                        turn = (gen_block + k) * 4 + f
+                        distances(jnp.minimum(turn + 1, (gen_block + count) * 4 - 1 if gen_block == 0 else 4 * NO - 1), (d2_b, d2_a)[h])
                         generate(gen_store, gen_slot + k, f, (d2_a, d2_b)[h], step_poly)
                 return inner
 
             lax.fori_loop(0, 2, half_step, 0)
-            if mm_store is not None and mm_turn < NO - 1:
+            if mm_store is not None and mm_block > 0:
                 for m in range(mm_count):
-                    part_copy(block_at(mm_turn + k * mm_count + m)).start()
+                    part_copy(mm_block + k * mm_count + m).start()
             return carry
 
         lax.fori_loop(0, count, block_step, 0)
@@ -283,17 +282,25 @@
     row = lax.broadcasted_iota(jnp.int32, (PAN, PAN), 0)
     col = lax.broadcasted_iota(jnp.int32, (PAN, PAN), 1)
     source = (row & 15) * 32 + ((row >> 5) & 3) * 8 + (row >> 7) * 2 + ((row >> 4) & 1)
-    perm[...] = (source == col).astype(F32).astype(BF16)
-
-    def await_place(step, carry):
-        place_copy(step).wait_send()
-        place_copy(NO - step).wait_recv()
-        spread(step)
+    perm = (source == col).astype(F32).astype(BF16)
+    for side in range(2):
+        store_b[0, side, 0:PAN, :] = perm[:, side * 256 : side * 256 + 256]
+
+    distances(jnp.int32(0), d2_a)
+    run(1, store_b, HELD // 2)
+
+    pl.semaphore_wait(barrier, NO - 1 + NF - 1)
+    start_all(place_copy)
+    start_all(spec_copy)
+    await_place(1)
+    distances(jnp.int32(4), d2_a)
+    run(HELD, store_a, 0, 1)
+
+    def await_rest(step, carry):
+        await_place(step)
         return carry
 
-    lax.fori_loop(1, NO, await_place, 0)
-    distances(jnp.int32(0), d2_a)
-    run(HELD, store_a)
+    lax.fori_loop(HELD + 2, NO, await_rest, 0)
 
     def await_spec(step, carry):
         spec_copy(step).wait_send()
@@ -311,7 +318,8 @@
     everything = spec_in[...].reshape(PAN, PAN)
     for f in range(BINS):
         wave = (q * BINS + (f + 1)).astype(F32) * 0.25 / kappa
-        rows = jnp.dot(perm[f * 128 : f * 128 + 128, :], everything, preferred_element_type=F32) * weight
+        perm = jnp.concatenate([store_b[0, side, f * 128 : f * 128 + 128, :] for side in range(2)], 1)
+        rows = jnp.dot(perm, everything, preferred_element_type=F32) * weight
         mono = turned(rows[0:32]) * wave
         load = [rows[32 * j + 32 : 32 * j + 64] for j in range(3)]
         load.append(-(load[0] * geo[0:1] + load[1] * geo[1:2] + load[2] * geo[2:3]))
@@ -323,15 +331,16 @@
                 [-turned(x) for x in side], 0
             ).astype(BF16)
 
-    run(4, store_b, 0, 8, store_a, 0, 2)
-    run(2, store_a, 0, 12, store_b, 8, 2)
-    run(1, store_b, 0, 14, store_a, 12, 2)
-    run(1, store_a, 0, 15, store_b, 14, 1)
-    run(1, mm_store=store_a, mm_turn=15)
+    run(4, store_b, 0, 9, store_a, 0, 1, 2)
+    run(2, store_a, 0, 13, store_b, 0, 9, 2)
+    run(1, store_b, 0, 15, store_a, 0, 13, 2)
+    run(1, mm_store=store_b, mm_slot=0, mm_block=15)
+    run(1, mm_store=store_b, mm_slot=HELD // 2, mm_block=0)
 
     out_ref[...] = part_out[0].astype(F32)
 
     def finish(step, carry):
+        place_copy(step).wait_send()
         part_copy(step).wait_send()
         part_copy(NO - step).wait_recv()
         out_ref[...] += part_in[step].astype(F32)
@@ -354,15 +363,14 @@
             pltpu.VMEM((PAN, 128), BF16),
             pltpu.VMEM((NO, 8, OBS), F32),
             pltpu.VMEM((NO, 8, OBS), F32),
-            pltpu.VMEM((NO, 128, OBS), BF16),
+            pltpu.VMEM((NO, 64, OBS), BF16),
             pltpu.VMEM((128, OBS), F32),
             pltpu.VMEM((128, OBS), F32),
             pltpu.VMEM((NF, 32, PAN), BF16),
             pltpu.VMEM((NF, 32, PAN), BF16),
-            pltpu.VMEM((PAN, PAN), BF16),
             pltpu.VMEM((BINS, GROUPS, ROWS), BF16),
             pltpu.VMEM((HELD, BINS, ROWS, OBS), BF16),
-            pltpu.VMEM((HELD // 2, BINS, ROWS, OBS), BF16),
+            pltpu.VMEM((HELD // 2 + 1, BINS, ROWS, OBS), BF16),
             pltpu.VMEM((NO, 128, OBS), BF16),
             pltpu.VMEM((NO, 128, OBS), BF16),
             dma((NO,)),
@@ -373,7 +381,7 @@
             dma((NO,)),
         ],
         compiler_params=pltpu.CompilerParams(
-            collective_id=0, has_side_effects=True, vmem_limit_bytes=60 * 2**20
+            collective_id=0, has_side_effects=True, vmem_limit_bytes=63 * 2**20
         ),
     )(jnp.asarray(dft_table()), samples, panel_geom, panel_slot, observer_pos, observer_slot)
     return out.reshape(BINS, 2, NF, OBS).transpose(3, 0, 1, 2)

time: 59.3 us -> 58.8 us (level)
  Pallas kernels: 57.4 us -> 56.6 us
    pallas_call x1, Pallas kernels: 57.4 us -> 56.6 us  [local(): pl.pallas_call(kernel, out_shape=jax.ShapeDtypeStruct((BINS * 2 * NF, OBS...]
where the time goes in v3:
time: 58.8 us; the launch traced here: 58.2 us
  Pallas kernels  56.6 us (96%)
  local copies, waits for them, and re-layouts  1.57 us (3%)
    pallas_call x1, Pallas kernels, local(): pl.pallas_call(kernel, out_shape=jax.ShapeDtypeStruct((BINS * 2 * NF, OBS...  56.6 us
    unnamed x1, local copies, waits for them, and re-layouts  1.57 us

profile of v3, /device:TPU:1, one launch (start us, length us, event | category | flops | bytes accessed | tf_op | source)
XLA Modules:
  0.0 58.2 jit_solution(751142144994158341)
XLA Ops:
  0.0 56.6 %shard_map.64 = f32[128,256]{1,0:T(8,128)} custom-call(bf16[128,128]{1,0:T(8,128)(2,1)} %constant.2.clone.table_ref, bf16[4,128,512]{2,1,0:T(8,128)(2,1)} %samples_ref.1, f32[4,512]{1,0:T(4,128)} %geom_ref.1, s32[1,512]{1,0:T(1,128)} %slot_ref.1, f32[3,256]{1,0:T(4,128)} %pos_ref.1, s32[1,256]{1,0:T(1,128)} %pos_slot_ref.1), custom_call_target="tpu_custom_call" | custom-call | tf_op jit(solution)/shard_map/pallas_call | solution.py:355
  56.6 1.6 %copy.8 = f32[256,4,2,16]{0,3,2,1:T(8,128)} copy(f32[256,4,2,16]{0,3,2,1:T(8,128)} %bitcast.3) | data formatting | bytes 262144

commit v4 on v3

--- a/solution.py
+++ b/solution.py
@@ -129,8 +129,7 @@
     place_in,
     place,
     right,
-    d2_a,
-    d2_b,
+    d2_ref,
     spec_out,
     spec_in,
     rhs_ref,
@@ -195,7 +194,7 @@
 
     def start_all(copy):
         def one(step, carry):
-            copy(step).start()
+            copy(NO - step).start()
             return carry
 
         lax.fori_loop(1, NO, one, 0)
@@ -231,10 +230,10 @@
         one, two, three = pieces(place[block])
         right[block] = jnp.concatenate([one, one, two, one, two, three, jnp.zeros((16, OBS), F32)], 0).astype(BF16)
 
-    def distances(turn, d2_ref):
-        block, quarter = turn // 4, lax.rem(turn, 4)
+    def distances(turn):
+        block, half = turn // 2, lax.rem(turn, 2)
         d2_ref[...] = jnp.dot(
-            left[pl.ds(pl.multiple_of(quarter * 128, 128), 128), 0:64], right[block], preferred_element_type=F32
+            left[pl.ds(pl.multiple_of(half * 256, 256), 256), 0:64], right[block], preferred_element_type=F32
         )
 
     inverse_square = 1.0 / (kappa * kappa)
@@ -264,9 +263,10 @@
                             result = contract(mm_store, mm_slot + at, f, rhs_ref, place, mm_block + at)
                             part_out[mm_block + at, pl.ds(pl.multiple_of(f * 32, 32), 32), :] = result.astype(BF16)
                     if gen_store is not None:
-                        turn = (gen_block + k) * 4 + f
-                        distances(jnp.minimum(turn + 1, (gen_block + count) * 4 - 1 if gen_block == 0 else 4 * NO - 1), (d2_b, d2_a)[h])
-                        generate(gen_store, gen_slot + k, f, (d2_a, d2_b)[h], step_poly)
+                        generate(gen_store, gen_slot + k, f, d2_ref.at[h * 128:h * 128 + 128], step_poly)
+                if gen_store is not None:
+                    turn = (gen_block + k) * 2 + half
+                    distances(jnp.minimum(turn + 1, 1 if gen_block == 0 else 2 * NO - 1))
                 return inner
 
             lax.fori_loop(0, 2, half_step, 0)
@@ -286,14 +286,14 @@
     for side in range(2):
         store_b[0, side, 0:PAN, :] = perm[:, side * 256 : side * 256 + 256]
 
-    distances(jnp.int32(0), d2_a)
+    distances(jnp.int32(0))
     run(1, store_b, HELD // 2)
 
     pl.semaphore_wait(barrier, NO - 1 + NF - 1)
     start_all(place_copy)
     start_all(spec_copy)
     await_place(1)
-    distances(jnp.int32(4), d2_a)
+    distances(jnp.int32(2))
     run(HELD, store_a, 0, 1)
 
     def await_rest(step, carry):
@@ -339,7 +339,8 @@
 
     out_ref[...] = part_out[0].astype(F32)
 
-    def finish(step, carry):
+    def finish(count, carry):
+        step = NO - count
         place_copy(step).wait_send()
         part_copy(step).wait_send()
         part_copy(NO - step).wait_recv()
@@ -364,8 +365,7 @@
             pltpu.VMEM((NO, 8, OBS), F32),
             pltpu.VMEM((NO, 8, OBS), F32),
             pltpu.VMEM((NO, 64, OBS), BF16),
-            pltpu.VMEM((128, OBS), F32),
-            pltpu.VMEM((128, OBS), F32),
+            pltpu.VMEM((256, OBS), F32),
             pltpu.VMEM((NF, 32, PAN), BF16),
             pltpu.VMEM((NF, 32, PAN), BF16),
             pltpu.VMEM((BINS, GROUPS, ROWS), BF16),

time: 58.8 us -> 54 us (0.918)
  Pallas kernels: 56.6 us -> 52.3 us
    pallas_call x1, Pallas kernels: 56.6 us -> 52.3 us  [local(): pl.pallas_call(kernel, out_shape=jax.ShapeDtypeStruct((BINS * 2 * NF, OBS...]
where the time goes in v4:
time: 54 us; the launch traced here: 53.8 us
  Pallas kernels  52.3 us (97%)
  local copies, waits for them, and re-layouts  1.57 us (3%)
    pallas_call x1, Pallas kernels, local(): pl.pallas_call(kernel, out_shape=jax.ShapeDtypeStruct((BINS * 2 * NF, OBS...  52.3 us
    unnamed x1, local copies, waits for them, and re-layouts  1.57 us

profile of v4, /device:TPU:1, one launch (start us, length us, event | category | flops | bytes accessed | tf_op | source)
XLA Modules:
  0.0 53.8 jit_solution(3731745458237876669)
XLA Ops:
  0.0 52.3 %shard_map.64 = f32[128,256]{1,0:T(8,128)} custom-call(bf16[128,128]{1,0:T(8,128)(2,1)} %constant.2.clone.table_ref, bf16[4,128,512]{2,1,0:T(8,128)(2,1)} %samples_ref.1, f32[4,512]{1,0:T(4,128)} %geom_ref.1, s32[1,512]{1,0:T(1,128)} %slot_ref.1, f32[3,256]{1,0:T(4,128)} %pos_ref.1, s32[1,256]{1,0:T(1,128)} %pos_slot_ref.1), custom_call_target="tpu_custom_call" | custom-call | tf_op jit(solution)/shard_map/pallas_call | solution.py:356
  52.3 1.6 %copy.8 = f32[256,4,2,16]{0,3,2,1:T(8,128)} copy(f32[256,4,2,16]{0,3,2,1:T(8,128)} %bitcast.3) | data formatting | bytes 262144

commit v5 on v4

--- a/solution.py
+++ b/solution.py
@@ -192,12 +192,12 @@
             device_id_type=MESH,
         )
 
-    def start_all(copy):
+    def start_all(copy, first=1, last=NO):
         def one(step, carry):
             copy(NO - step).start()
             return carry
 
-        lax.fori_loop(1, NO, one, 0)
+        lax.fori_loop(first, last, one, 0)
 
     for c in range(0, CH, 2):
         pair = [
@@ -290,8 +290,9 @@
     run(1, store_b, HELD // 2)
 
     pl.semaphore_wait(barrier, NO - 1 + NF - 1)
-    start_all(place_copy)
+    start_all(place_copy, 1, 4)
     start_all(spec_copy)
+    start_all(place_copy, 4, NO)
     await_place(1)
     distances(jnp.int32(2))
     run(HELD, store_a, 0, 1)

time: 54 us -> 54 us (level)
  no operation moved by 1% of the time
where the time goes in v5:
time: 54 us; the launch traced here: 53.8 us
  Pallas kernels  52.3 us (97%)
  local copies, waits for them, and re-layouts  1.57 us (3%)
    pallas_call x1, Pallas kernels, local(): pl.pallas_call(kernel, out_shape=jax.ShapeDtypeStruct((BINS * 2 * NF, OBS...  52.3 us
    unnamed x1, local copies, waits for them, and re-layouts  1.57 us

profile of v5, /device:TPU:1, one launch (start us, length us, event | category | flops | bytes accessed | tf_op | source)
XLA Modules:
  0.0 53.8 jit_solution(321466800599202073)
XLA Ops:
  0.0 52.3 %shard_map.64 = f32[128,256]{1,0:T(8,128)} custom-call(bf16[128,128]{1,0:T(8,128)(2,1)} %constant.2.clone.table_ref, bf16[4,128,512]{2,1,0:T(8,128)(2,1)} %samples_ref.1, f32[4,512]{1,0:T(4,128)} %geom_ref.1, s32[1,512]{1,0:T(1,128)} %slot_ref.1, f32[3,256]{1,0:T(4,128)} %pos_ref.1, s32[1,256]{1,0:T(1,128)} %pos_slot_ref.1), custom_call_target="tpu_custom_call" | custom-call | tf_op jit(solution)/shard_map/pallas_call | solution.py:357
  52.3 1.6 %copy.8 = f32[256,4,2,16]{0,3,2,1:T(8,128)} copy(f32[256,4,2,16]{0,3,2,1:T(8,128)} %bitcast.3) | data formatting | bytes 262144
